TPU v7x, 128 devices: a whole 4x4x4 slice. The times are simulated.
128 devices in a mesh: dp: 32 (over x, y, core), space: 4 (over z).
Axes of the slice: x: 4, y: 4, z: 4, core: 2. Of those that a mesh axis runs over, the one named last changes fastest.
Arguments:
- features: bfloat16 [32, 8, 128, 512], P('dp', 'space'), may hold values from -6 to 6
- latent_bank: float32 [1024, 512], replicated, may hold values from -6 to 6
- latent_ids: int32 [32], P('dp'), may hold values from 0 to 1023
- conv_kernel: bfloat16 [3, 3, 512, 512], P(None, None, 'dp'), may hold values from -0.09375 to 0.09375
- style_one: float32 [512, 512], replicated, may hold values from -0.25 to 0.25
- bias_one: float32 [512], replicated, may hold values from 0.1 to 1.9
- style_two: float32 [512, 512], replicated, may hold values from -0.25 to 0.25
- bias_two: float32 [512], replicated, may hold values from 0.1 to 1.9
- rgb_weight: float32 [512, 3], replicated, may hold values from -0.25 to 0.25
- conv_bias: float32 [512], replicated, may hold values from -3 to 3
- direction: float32 [32, 3, 8, 128], P('dp', None, 'space'), may hold values from -60 to 60
- length_target: float32 [1], replicated, may hold values from 0.5 to 3
Outputs:
- kernel_grad: float32 [3, 3, 512, 512], P(None, None, 'dp')
- path_lengths: float32 [32], P('dp')
- new_target: float32 [1], replicated
All inputs are finite; a program needn't handle non-finite values.
Results may differ from a plain program's by a relative error of at most 0.025.
Values may be sent and summed in bfloat16 or wider, within the bound.
No kernel may reach another device: no remote copies, remote signals or barrier semaphores. Data moves between devices by JAX's collectives and lax.ppermute only.
A program may use at most 64 MiB of HBM per device.

v0:
```python
import math
import jax
import jax.numpy as jnp
from jax import lax
from jax.sharding import PartitionSpec as P

PL_WEIGHT = 8.0
PL_DECAY = 0.5
SQRT_TWO = math.sqrt(2.0)
HIGHEST = lax.Precision.HIGHEST


def extended(block, sides, width):
    for axis, dim in sides:
        count = lax.axis_size(axis)
        forward = [(i, i + 1) for i in range(count - 1)]
        backward = [(target, source) for source, target in forward]
        low = lax.ppermute(
            lax.slice_in_dim(block, block.shape[dim] - width, None, axis=dim), axis, forward
        )
        high = lax.ppermute(lax.slice_in_dim(block, 0, width, axis=dim), axis, backward)
        block = jnp.concatenate([low, block, high], axis=dim)
    return block


def synth(padded, latent, kernel_full, params, target_dir, scaling):
    style_one, bias_one, style_two, bias_two, rgb_weight, conv_bias = params
    tile_rows = padded.shape[0] - 2
    tile_cols = padded.shape[1] - 2
    channels = padded.shape[2]
    style_in = jnp.dot(latent, style_one, precision=HIGHEST) + bias_one
    energy = jnp.sum(kernel_full * kernel_full, axis=(0, 1))
    demodulation = lax.rsqrt(jnp.dot(style_in * style_in, energy, precision=HIGHEST) + 1e-08)
    modulated = (
        kernel_full * style_in[None, None, :, None] * demodulation[None, None, None, :]
    ).astype(jnp.bfloat16)
    hidden = jnp.zeros((tile_rows * tile_cols, modulated.shape[3]), jnp.float32) + conv_bias
    for row_off in range(3):
        for col_off in range(3):
            window = padded[row_off : row_off + tile_rows, col_off : col_off + tile_cols].reshape(
                tile_rows * tile_cols, channels
            )
            hidden = hidden + jnp.dot(
                window, modulated[row_off, col_off], preferred_element_type=jnp.float32
            )
    activated = ((0.6 * hidden + 0.4 * jnp.sqrt(hidden * hidden + 0.25)) * SQRT_TWO).astype(
        jnp.bfloat16
    )
    colour = jnp.dot(latent, style_two, precision=HIGHEST) + bias_two
    rgb_mod = (rgb_weight * colour[:, None]).astype(jnp.bfloat16)
    picture = jnp.dot(activated, rgb_mod, preferred_element_type=jnp.float32)
    return jnp.sum(picture * target_dir.reshape(3, tile_rows * tile_cols).T) * scaling


def per_device(
    features,
    latent_bank,
    latent_ids,
    conv_kernel,
    style_one,
    bias_one,
    style_two,
    bias_two,
    rgb_weight,
    conv_bias,
    direction,
    length_target,
):
    kernel_whole = lax.all_gather(conv_kernel, "dp", axis=2, tiled=True)
    kernel_full = kernel_whole.astype(jnp.float32)
    bordered = extended(features, (("space", 1),), 1)
    padded = jnp.pad(bordered, ((0, 0), (0, 0), (1, 1), (0, 0)))
    latents = jnp.take(latent_bank, latent_ids, axis=0)
    scaling = 1.0 / math.sqrt(features.shape[1] * lax.axis_size("space") * features.shape[2])
    params = (style_one, bias_one, style_two, bias_two, rgb_weight, conv_bias)

    def one_grad(pad_one, latent, dir_one):
        return jax.grad(synth, argnums=1)(pad_one, latent, kernel_full, params, dir_one, scaling)

    partial_grads = jax.vmap(one_grad)(padded, latents, direction)
    style_grads = lax.psum(partial_grads, "space")
    lengths = jnp.sqrt(jnp.sum(style_grads * style_grads, axis=1) + 1e-08)
    total = lax.psum(jnp.sum(lengths), "dp")
    target = length_target + PL_DECAY * (
        total / (lengths.shape[0] * lax.axis_size("dp")) - length_target
    )
    factor = 2.0 * PL_WEIGHT * (lengths - target) / lengths
    tangents = factor[:, None] * style_grads

    def total_of(kernel_var):

        def along(pad_one, latent, tangent, dir_one):
            return jax.jvp(
                lambda point: synth(pad_one, point, kernel_var, params, dir_one, scaling),
                (latent,),
                (tangent,),
            )[1]

        return jnp.sum(jax.vmap(along)(padded, latents, tangents, direction))

    kernel_sum = jax.grad(total_of)(kernel_full)
    shard_sum = lax.psum_scatter(
        kernel_sum.astype(jnp.bfloat16), "dp", scatter_dimension=2, tiled=True
    )
    kernel_grad = lax.psum(shard_sum, "space").astype(jnp.float32)
    return (kernel_grad, lengths, target)


def solution(mesh):
    in_specs = (
        P("dp", "space", None, None),
        P(),
        P("dp"),
        P(None, None, "dp", None),
        P(),
        P(),
        P(),
        P(),
        P(),
        P(),
        P("dp", None, "space", None),
        P(),
    )
    out_specs = (P(None, None, "dp", None), P("dp"), P())
    return jax.shard_map(
        per_device, mesh=mesh, in_specs=in_specs, out_specs=out_specs, check_vma=False
    )
```

profile of v0, /device:TPU:0, one launch (start us, length us, event | category | flops | bytes accessed | tf_op | source)
XLA Modules:
  0.0 311.9 jit_solution(5924090728413507393)
XLA Ops:
  7.2 0.7 all-gather.2.cloned.1.call-update
  8.0 1.0 fusion.108
  9.0 3.9 %collective-permute-start = (bf16[1,1,128,512]{3,2,1,0:T(8,128)(2,1)S(1)}, bf16[1,1,128,512]{3,2,1,0:T(8,128)(2,1)S(1)}, u32[]{:S(2)}, u32[]{:S(2)}) collective-permute-start(bf16[1,1,128,512]{3,2,1,0:T(8,128)(2,1)S(1)} %get-tuple-element.29), channel_id=1, source_target_pairs={{0,1},{1,2},{2,3},{4,5},{5,6},{6,7},{8,9},{9,10},{10,11},{12,13},{... | collective-permute-start | bytes 393224 | tf_op jit(solution)/shard_map/ppermute | solution.py:18
  12.9 1.3 collective-permute-start.1
  14.8 1.3 fusion.100
  16.2 0.7 add.176
  16.9 0.7 broadcast_multiply_fusion
  17.5 1.8 fusion.49
  19.3 1.8 fusion.102
  21.2 0.7 fusion.106
  21.9 1.8 pad_maximum_fusion
  23.7 1.1 fusion.61
  24.8 1.0 fusion.107
  25.8 33.8 %all-gather.2.cloned.1.call-done = bf16[3,3,512,512]{3,2,1,0:T(8,128)(2,1)} async-done(((bf16[3,3,16,512]{3,2,1,0:T(8,128)(2,1)}), bf16[3,3,512,512]{3,2,1,0:T(8,128)(2,1)}) %all-gather.2.cloned.1.call-update) | async-done | bytes 4718608 | tf_op jit(solution)/shard_map/all_gather | solution.py:69
  59.6 3.5 %fusion.19 = f32[512,512]{1,0:T(8,128)S(1)} fusion(bf16[3,3,512,512]{3,2,1,0:T(8,128)(2,1)} %all-gather.2.cloned.1.call-done), kind=kLoop, calls=%fused_computation.31 | loop fusion | flops 6815744 | bytes 5767168 | tf_op jit(solution)/shard_map/jvp(vmap(jvp()))/reduce_sum | solution.py:32
  63.1 0.6 fusion.109
  63.8 1.3 fusion.20
  65.7 0.3 fusion.69
  66.3 0.3 convolution_add_fusion.7
  66.7 0.3 fusion.48
  67.0 0.3 convolution_add_fusion.5
  67.3 0.3 fusion.42
  67.6 0.6 multiply_add_fusion.1
  68.2 0.3 fusion.22
  68.6 0.3 fusion.24
  68.9 0.3 fusion.25
  69.3 0.3 fusion.27
  69.6 0.3 fusion.23
  70.0 0.3 fusion.28
  70.3 0.3 fusion.29
  70.7 0.3 fusion.26
  71.0 0.3 fusion.30
  71.4 5.6 %fusion.17 = (f32[512]{0:T(512)S(1)}, f32[512]{0:T(512)S(1)}, bf16[1,3,3,512,512]{4,3,2,1,0:T(8,128)(2,1)}) fusion(bf16[3,3,512,512]{3,2,1,0:T(8,128)(2,1)S(1)} %copy-done.1, f32[512]{0:T(512)S(1)} %get-tuple-element.20, f32[512]{0:T(512)S(1)} %add_rsqrt_fusion, bf16[1,1,1,512,512]{4,3,2,1,0:T(8,128)(2,1)S(1)} %fusion.30, ...), kind=kLoop, calls=%fused_computation.29 | loop fusion | flops 37747712 | bytes 14163968 | tf_op jit(solution)/shard_map/vmap(transpose(jvp()))/reduce_sum | solution.py:35
  77.0 1.0 fusion.111
  78.0 1.0 fusion.112
  79.0 0.4 fusion.56
  79.4 1.0 fusion.110
  80.3 10.7 %psum.21 = f32[1,512]{1,0:T(1,128)S(1)} all-reduce(f32[1,512]{1,0:T(1,128)S(1)} %bitcast.414), channel_id=1, replica_groups=mesh['dp'=32,'space'=4] {'space'}, use_global_device_ids=true, to_apply=%region_4.5 | all-reduce | flops 512 | bytes 4096 | tf_op jit(solution)/shard_map/psum | solution.py:81
  91.0 0.6 multiply_reduce_fusion
  93.0 64.2 %psum.22 = f32[]{:T(128)} all-reduce(f32[]{:T(128)} %sqrt.12), channel_id=1, replica_groups=mesh['dp'=32,'space'=4] {'dp'}, use_global_device_ids=true, to_apply=%region_6.7 | all-reduce | flops 1 | bytes 8 | tf_op jit(solution)/shard_map/psum | solution.py:83
  157.9 0.6 fusion.88
  158.5 0.6 fusion.90
  159.1 0.6 fusion.113
  159.8 4.7 %fusion.21 = bf16[1,3,3,512,512]{4,3,2,1,0:T(8,128)(2,1)S(1)} fusion(bf16[3,3,512,512]{3,2,1,0:T(8,128)(2,1)} %all-gather.2.cloned.1.call-done, f32[512]{0:T(512)S(1)} %fusion.104, f32[512]{0:T(512)S(1)} %bitcast.396, f32[512]{0:T(512)S(1)} %add_rsqrt_fusion, f32[512]{0:T(512)S(1)} %get-tuple-element.20), kind=kLoop, calls=%fused_computation.33 | loop fusion | flops 16515072 | bytes 9445376 | tf_op jit(solution)/shard_map/jvp(vmap(jvp()))/convert_element_type | solution.py:36
  165.4 0.3 fusion.63
  166.0 0.3 convolution_add_fusion.3
  166.3 0.3 convolution_add_fusion.2
  166.7 0.3 convolution_add_fusion.1
  167.0 0.3 fusion.45
  167.3 0.8 fusion.62
  168.1 0.4 fusion.31
  168.5 0.4 fusion.33
  168.8 0.4 fusion.34
  169.2 0.3 fusion.36
  169.5 0.3 fusion.32
  169.9 0.3 fusion.37
  170.2 0.4 fusion.38
  170.6 0.4 fusion.35
  170.9 0.4 fusion.39
  171.4 3.1 fusion.14
  174.7 5.6 %fusion.16 = bf16[3,3,512,512]{3,2,1,0:T(8,128)(2,1)} fusion(bf16[1,3,3,512,512]{4,3,2,1,0:T(8,128)(2,1)S(1)} %bitcast.354, bf16[3,3,512,512]{3,2,1,0:T(8,128)(2,1)S(1)} %bitcast.352, f32[512,512]{1,0:T(8,128)S(1)} %multiply_add_fusion, f32[512]{0:T(512)S(1)} %get-tuple-element.20, f32[512]{0:T(512)S(1)} %fusion.104, f32[512]{0:T(512)S(1)} %bitcast.398, ...), kind=kLoop, calls=%fused_computation.28 | loop fusion | flops 51904512 | bytes 19931136 | tf_op jit(solution)/shard_map/convert_element_type | solution.py:103
  180.3 77.7 %reduce-scatter.2.cloned.1.call-done = bf16[3,3,16,512]{3,2,1,0:T(8,128)(2,1)} async-done(((bf16[3,3,512,512]{3,2,1,0:T(8,128)(2,1)}), bf16[3,3,16,512]{3,2,1,0:T(8,128)(2,1)}) %reduce-scatter.2.cloned.1.call-update) | async-done | bytes 147472 | tf_op jit(solution)/shard_map/reduce_scatter | solution.py:102
  258.1 43.3 %all-reduce.21.cloned.1.call-done = bf16[3,3,16,512]{3,2,1,0:T(8,128)(2,1)} async-done(((bf16[3,3,16,512]{3,2,1,0:T(8,128)(2,1)}), bf16[3,3,16,512]{3,2,1,0:T(8,128)(2,1)}) %all-reduce.21.cloned.1.call-update) | async-done | bytes 147472 | tf_op jit(solution)/shard_map/psum | solution.py:105
  301.4 1.7 convert_element_type.320
  (84 shorter events, 2.6 us)
Async XLA Ops:
  7.2 7.7 %copy-start = (f32[512,512]{1,0:T(8,128)S(1)}, f32[512,512]{1,0:T(8,128)}, u32[]{:S(2)}) copy-start(f32[512,512]{1,0:T(8,128)} %param.18) | copy-start | bytes 3145732
  7.2 52.4 %all-gather.2.cloned.1.call-start = ((), (), s32[]{:S(2)}) async-start(), calls=%async_computation.1 | async-start | bytes 4866048 | tf_op jit(solution)/shard_map/all_gather | solution.py:69
  7.9 250.1 %reduce-scatter.2.cloned.1.call-start = ((), (), s32[]{:S(2)}) async-start(), calls=%async_computation.2 | async-start | bytes 4866048 | tf_op jit(solution)/shard_map/reduce_scatter | solution.py:102
  9.0 12.9 %collective-permute-start = (bf16[1,1,128,512]{3,2,1,0:T(8,128)(2,1)S(1)}, bf16[1,1,128,512]{3,2,1,0:T(8,128)(2,1)S(1)}, u32[]{:S(2)}, u32[]{:S(2)}) collective-permute-start(bf16[1,1,128,512]{3,2,1,0:T(8,128)(2,1)S(1)} %get-tuple-element.29), channel_id=1, source_target_pairs={{0,1},{1,2},{2,3},{4,5},{5,6},{6,7},{8,9},{9,10},{10,11},{12,13},{... | collective-permute-start | bytes 393224 | tf_op jit(solution)/shard_map/ppermute | solution.py:18
  12.9 9.0 %collective-permute-start.1 = (bf16[1,1,128,512]{3,2,1,0:T(8,128)(2,1)S(1)}, bf16[1,1,128,512]{3,2,1,0:T(8,128)(2,1)S(1)}, u32[]{:S(2)}, u32[]{:S(2)}) collective-permute-start(bf16[1,1,128,512]{3,2,1,0:T(8,128)(2,1)S(1)} %get-tuple-element.30), channel_id=1, source_target_pairs={{1,0},{2,1},{3,2},{5,4},{6,5},{7,6},{9,8},{10,9},{11,10},{13,12},{... | collective-permute-start | bytes 393224 | tf_op jit(solution)/shard_map/ppermute | solution.py:21
  25.7 43.2 %copy-start.10 = (bf16[1,2,128,512]{3,2,1,0:T(8,128)(2,1)}, bf16[1,2,128,512]{3,2,1,0:T(8,128)(2,1)S(1)}, u32[]{:S(2)}) copy-start(bf16[1,2,128,512]{3,2,1,0:T(8,128)(2,1)S(1)} %get-tuple-element.23) | copy-start | bytes 786436
  25.7 43.5 %copy-start.8 = (bf16[1,2,128,512]{3,2,1,0:T(8,128)(2,1)}, bf16[1,2,128,512]{3,2,1,0:T(8,128)(2,1)S(1)}, u32[]{:S(2)}) copy-start(bf16[1,2,128,512]{3,2,1,0:T(8,128)(2,1)S(1)} %get-tuple-element.21) | copy-start | bytes 786436
  25.7 44.2 %copy-start.6 = (bf16[1,2,128,512]{3,2,1,0:T(8,128)(2,1)}, bf16[1,2,128,512]{3,2,1,0:T(8,128)(2,1)S(1)}, u32[]{:S(2)}) copy-start(bf16[1,2,128,512]{3,2,1,0:T(8,128)(2,1)S(1)} %get-tuple-element.24) | copy-start | bytes 786436
  25.7 45.3 %copy-start.4 = (bf16[1,2,128,512]{3,2,1,0:T(8,128)(2,1)}, bf16[1,2,128,512]{3,2,1,0:T(8,128)(2,1)S(1)}, u32[]{:S(2)}) copy-start(bf16[1,2,128,512]{3,2,1,0:T(8,128)(2,1)S(1)} %get-tuple-element.25) | copy-start | bytes 786436
  59.6 4.1 %copy-start.1 = (bf16[3,3,512,512]{3,2,1,0:T(8,128)(2,1)S(1)}, bf16[3,3,512,512]{3,2,1,0:T(8,128)(2,1)}, u32[]{:S(2)}) copy-start(bf16[3,3,512,512]{3,2,1,0:T(8,128)(2,1)} %all-gather.2.cloned.1.call-done) | copy-start | bytes 14155780
  63.7 1.6 copy-start.12
  63.7 2.3 copy-start.14
  65.0 1.3 copy-start.23
  65.1 1.6 copy-start.16
  65.4 1.9 copy-start.2
  66.0 1.6 copy-start.18
  66.0 1.6 copy-start.20
  68.2 10.8 %copy-start.24 = (f32[256,512]{1,0:T(8,128)}, f32[256,512]{1,0:T(8,128)S(1)}, u32[]{:S(2)}) copy-start(f32[256,512]{1,0:T(8,128)S(1)} %get-tuple-element.32) | copy-start | bytes 1572868
  71.4 6.6 %copy-start.3 = (f32[512,512]{1,0:T(8,128)S(1)}, f32[512,512]{1,0:T(8,128)}, u32[]{:S(2)}) copy-start(f32[512,512]{1,0:T(8,128)} %param.16) | copy-start | bytes 3145732
  71.4 7.6 %copy-start.22 = (f32[512,3]{0,1:T(4,128)S(1)}, f32[512,3]{0,1:T(4,128)}, u32[]{:S(2)}) copy-start(f32[512,3]{0,1:T(4,128)} %param.20) | copy-start | bytes 18436
  159.7 4.7 %copy-start.5 = (bf16[1,2,128,512]{3,2,1,0:T(8,128)(2,1)S(1)}, bf16[1,2,128,512]{3,2,1,0:T(8,128)(2,1)}, u32[]{:S(2)}) copy-start(bf16[1,2,128,512]{3,2,1,0:T(8,128)(2,1)} %copy-done.4) | copy-start | bytes 786436
  159.7 5.0 %copy-start.11 = (bf16[1,2,128,512]{3,2,1,0:T(8,128)(2,1)S(1)}, bf16[1,2,128,512]{3,2,1,0:T(8,128)(2,1)}, u32[]{:S(2)}) copy-start(bf16[1,2,128,512]{3,2,1,0:T(8,128)(2,1)} %copy-done.10) | copy-start | bytes 786436
  159.8 5.3 %copy-start.13 = (bf16[1,2,128,512]{3,2,1,0:T(8,128)(2,1)S(1)}, bf16[1,2,128,512]{3,2,1,0:T(8,128)(2,1)}, u32[]{:S(2)}) copy-start(bf16[1,2,128,512]{3,2,1,0:T(8,128)(2,1)} %get-tuple-element.22) | copy-start | bytes 786436
  159.8 5.6 %copy-start.15 = (bf16[1,2,128,512]{3,2,1,0:T(8,128)(2,1)S(1)}, bf16[1,2,128,512]{3,2,1,0:T(8,128)(2,1)}, u32[]{:S(2)}) copy-start(bf16[1,2,128,512]{3,2,1,0:T(8,128)(2,1)} %get-tuple-element.26) | copy-start | bytes 786436
  164.4 1.6 copy-start.17
  164.5 1.9 copy-start.7
  164.5 2.2 copy-start.9
  165.7 1.6 copy-start.19
  165.7 1.6 copy-start.21
  165.7 1.6 copy-start.25
  167.3 4.0 %slice-start = ((s8[4718592]{0:T(1024)(128)(4,1)}), s8[4194304]{0:T(1024)(128)(4,1)S(1)}, s32[]{:S(2)}) async-start(s8[4718592]{0:T(1024)(128)(4,1)} %bitcast.351), calls=%async_computation.4 | async-start | bytes 8388608
  167.3 4.0 %slice-start.2 = ((s8[4718592]{0:T(1024)(128)(4,1)}), s8[4194304]{0:T(1024)(128)(4,1)S(1)}, s32[]{:S(2)}) async-start(s8[4718592]{0:T(1024)(128)(4,1)} %bitcast.353), calls=%async_computation.6 | async-start | bytes 8388608
  168.1 3.2 %slice-start.1 = ((s8[4718592]{0:T(1024)(128)(4,1)}), s8[524288]{0:T(1024)(128)(4,1)S(1)}, s32[]{:S(2)}) async-start(s8[4718592]{0:T(1024)(128)(4,1)} %bitcast.351), calls=%async_computation.5 | async-start | bytes 1048576
  168.1 3.2 %slice-start.3 = ((s8[4718592]{0:T(1024)(128)(4,1)}), s8[524288]{0:T(1024)(128)(4,1)S(1)}, s32[]{:S(2)}) async-start(s8[4718592]{0:T(1024)(128)(4,1)} %bitcast.353), calls=%async_computation.7 | async-start | bytes 1048576
  180.3 121.2 %all-reduce.21.cloned.1.call-start = ((), (), s32[]{:S(2)}) async-start(), calls=%async_computation.3 | async-start | bytes 294912 | tf_op jit(solution)/shard_map/psum | solution.py:105
Sparse Core Ops, SparseCore 0:
  10.4 49.1 all-gather.1
  180.4 77.6 reduce-scatter.1
  260.5 40.8 all-reduce.20
where the time goes:
time: 312 us
  waiting for transfers between devices  156 us (50%)
  blocking collectives  74.9 us (24%)
  other arithmetic  31.2 us (10%)
  matrix products  23.2 us (7%)
  between operations  19.4 us (6%)
  starting transfers between devices  5.32 us (2%)
    reduce_scatter x1, waiting for transfers between devices, per_device(): lax.psum_scatter(kernel_sum.astype(jnp.bfloat16), 'dp', scatter_dimension...  77.7 us
    psum x1, blocking collectives, per_device(): total = lax.psum(jnp.sum(lengths), 'dp')  64.2 us
    psum x1, waiting for transfers between devices, per_device(): kernel_grad = lax.psum(shard_sum, 'space').astype(jnp.float32)  43.3 us
    all_gather x1, waiting for transfers between devices, per_device(): kernel_whole = lax.all_gather(conv_kernel, 'dp', axis=2, tiled=True)  33.8 us
    dot_general x36, matrix products, synth(): jnp.dot(window, modulated[row_off, col_off], preferred_element_type=jnp.f...  12.3 us
    psum x1, blocking collectives, per_device(): style_grads = lax.psum(partial_grads, 'space')  10.7 us
    reduce_sum x2, other arithmetic, synth(): kernel_full * style_in[None, None, :, None]  8.7 us
  transfers between devices with their start and end apart: 5, of which 3 were waited for; matrix products, arithmetic and copies ran while one was open for 4% of the time, Pallas kernels for 0%

commit v1 on v0

--- a/solution.py
+++ b/solution.py
@@ -66,7 +66,13 @@
     direction,
     length_target,
 ):
-    kernel_whole = lax.all_gather(conv_kernel, "dp", axis=2, tiled=True)
+    take_seats_all_by_axis = lambda message, k_dim: jnp.concatenate(
+        lax.all_to_all(
+            jnp.stack([message for _ in range(lax.axis_size("dp"))], axis=0), "dp", 0, 0
+        ),
+        axis=k_dim,
+    )
+    kernel_whole = take_seats_all_by_axis(conv_kernel, 2)
     kernel_full = kernel_whole.astype(jnp.float32)
     bordered = extended(features, (("space", 1),), 1)
     padded = jnp.pad(bordered, ((0, 0), (0, 0), (1, 1), (0, 0)))

time: 312 us -> 348 us (1.12)
  waiting for transfers between devices: 156 us -> 168 us
  local copies, waits for them, and re-layouts: 2.12 us -> 9.85 us
  starting transfers between devices: 5.32 us -> 12.9 us
  other arithmetic: 31.2 us -> 37 us
    all_to_all x0 -> x1, waiting for transfers between devices: none -> 45.7 us  [per_device(): lax.all_to_all(jnp.stack([message for _ in range(lax.axis_size('dp'))], a...]
    all_gather x1 -> x0, waiting for transfers between devices: 33.8 us -> none  [per_device(): kernel_whole = lax.all_gather(conv_kernel, 'dp', axis=2, tiled=True)]
    all_to_all x0 -> x1, starting transfers between devices: none -> 7.66 us  [per_device(): lax.all_to_all(jnp.stack([message for _ in range(lax.axis_size('dp'))], a...]
    convert_element_type x0 -> x1, other arithmetic: none -> 7.36 us  [per_device(): kernel_full = kernel_whole.astype(jnp.float32)]
    convert_element_type x0 -> x1, local copies, waits for them, and re-layouts: none -> 4.79 us  [per_device(): kernel_full = kernel_whole.astype(jnp.float32)]
    another operation x0 -> x1, local copies, waits for them, and re-layouts: none -> 3.73 us  [per_device(): jnp.stack([message for _ in range(lax.axis_size('dp'))], axis=0)]
    reduce_sum x2 -> x3, other arithmetic: 8.7 us -> 5.96 us  [synth(): kernel_full * style_in[None, None, :, None]]
  transfers between devices with their start and end apart: 5 -> 5, of which waited for: 3 -> 4; matrix products, arithmetic and copies ran while one was open for 4% -> 2% of each run, Pallas kernels for 0% -> 0%
where the time goes in v1:
time: 348 us; the launch traced here: 347 us
  waiting for transfers between devices  168 us (48%)
  blocking collectives  75.7 us (22%)
  other arithmetic  37 us (11%)
  matrix products  23.2 us (7%)
  between operations  20 us (6%)
  starting transfers between devices  12.9 us (4%)
  local copies, waits for them, and re-layouts  9.85 us (3%)
    reduce_scatter x1, waiting for transfers between devices, per_device(): lax.psum_scatter(kernel_sum.astype(jnp.bfloat16), 'dp', scatter_dimension...  77.8 us
    psum x1, blocking collectives, per_device(): total = lax.psum(jnp.sum(lengths), 'dp')  63.9 us
    all_to_all x1, waiting for transfers between devices, per_device(): lax.all_to_all(jnp.stack([message for _ in range(lax.axis_size('dp'))], a...  45.7 us
    psum x1, waiting for transfers between devices, per_device(): kernel_grad = lax.psum(shard_sum, 'space').astype(jnp.float32)  43.3 us
    dot_general x36, matrix products, synth(): jnp.dot(window, modulated[row_off, col_off], preferred_element_type=jnp.f...  12.3 us
    psum x1, blocking collectives, per_device(): style_grads = lax.psum(partial_grads, 'space')  11.7 us
    convert_element_type x2, other arithmetic, synth(): modulated = (kernel_full * style_in[None, None, :, None] * demodulation[N...  8.93 us
    convert_element_type x1, other arithmetic, per_device(): kernel_sum.astype(jnp.bfloat16)  7.66 us
  transfers between devices with their start and end apart: 5, of which 4 were waited for; matrix products, arithmetic and copies ran while one was open for 2% of the time, Pallas kernels for 0%

profile of v1, /device:TPU:0, one launch (start us, length us, event | category | flops | bytes accessed | tf_op | source)
XLA Modules:
  0.0 347.0 jit_solution(13128364409742609452)
XLA Ops:
  7.2 3.7 %stack.2 = bf16[32,3,3,16,512]{4,3,2,1,0:T(8,128)(2,1)} broadcast(bf16[3,3,16,512]{3,2,1,0:T(8,128)(2,1)} %param.15), dimensions={1,2,3,4} | broadcast | bytes 4866048 | tf_op jit(solution)/shard_map/stack | solution.py:71
  10.9 7.7 %all-to-all-start = ((bf16[32,3,3,16,512]{4,3,2,1,0:T(8,128)(2,1)}), bf16[32,3,3,16,512]{4,3,2,1,0:T(8,128)(2,1)}, u32[]{:S(2)}, u32[]{:S(2)}) async-start(bf16[32,3,3,16,512]{4,3,2,1,0:T(8,128)(2,1)} %stack.2), calls=%async_computation | async-start | bytes 9437184 | tf_op jit(solution)/shard_map/all_to_all | solution.py:70
  18.7 3.8 %collective-permute-start = (bf16[1,1,128,512]{3,2,1,0:T(8,128)(2,1)S(1)}, bf16[1,1,128,512]{3,2,1,0:T(8,128)(2,1)S(1)}, u32[]{:S(2)}, u32[]{:S(2)}) collective-permute-start(bf16[1,1,128,512]{3,2,1,0:T(8,128)(2,1)S(1)} %get-tuple-element.26), channel_id=1, source_target_pairs={{0,1},{1,2},{2,3},{4,5},{5,6},{6,7},{8,9},{9,10},{10,11},{12,13},{... | collective-permute-start | bytes 393224 | tf_op jit(solution)/shard_map/ppermute | solution.py:18
  22.5 1.3 collective-permute-start.1
  24.5 1.3 fusion.90
  25.9 1.1 fusion.39
  27.0 1.3 fusion.92
  28.3 1.6 collective-permute-done.1
  29.9 0.9 pad_maximum_fusion
  31.0 1.0 fusion.97
  31.9 45.7 %all-to-all-done = bf16[32,3,3,16,512]{4,3,2,1,0:T(8,128)(2,1)} async-done(((bf16[32,3,3,16,512]{4,3,2,1,0:T(8,128)(2,1)}), bf16[32,3,3,16,512]{4,3,2,1,0:T(8,128)(2,1)}, u32[]{:S(2)}, u32[]{:S(2)}) %all-to-all-start) | async-done | bytes 4718624 | tf_op jit(solution)/shard_map/all_to_all | solution.py:70
  77.6 3.6 %fusion.8 = f32[32,16,512]{2,1,0:T(8,128)S(1)} fusion(bf16[32,3,3,16,512]{4,3,2,1,0:T(8,128)(2,1)} %all-to-all-done), kind=kLoop, calls=%fused_computation.17 | loop fusion | flops 6815744 | bytes 5767168 | tf_op jit(solution)/shard_map/jvp(vmap(jvp()))/reduce_sum | solution.py:32
  81.1 0.6 fusion.99
  81.7 7.4 %convert_bitcast_fusion = f32[3,3,32,16,512]{4,3,1,0,2:T(8,128)} fusion(bf16[32,3,3,16,512]{4,3,2,1,0:T(8,128)(2,1)} %all-to-all-done), kind=kLoop, calls=%fused_computation.6 | loop fusion | flops 2359296 | bytes 14155776 | tf_op jit(solution)/shard_map/convert_element_type | solution.py:76
  89.1 4.8 %copy.23 = f32[3,3,32,16,512]{4,3,2,1,0:T(8,128)S(1)} copy(f32[3,3,32,16,512]{4,3,1,0,2:T(8,128)} %convert_bitcast_fusion) | data formatting | bytes 18874368 | tf_op jit(solution)/shard_map/convert_element_type | solution.py:76
  93.9 1.6 multiply_convert_fusion
  95.6 0.3 fusion.60
  95.9 0.3 fusion.59
  96.9 0.3 convolution_add_fusion.7
  97.2 0.3 fusion.38
  97.5 0.3 convolution_add_fusion.5
  97.8 0.3 fusion.32
  98.3 0.6 multiply_add_fusion.1
  98.9 0.3 fusion.12
  99.2 0.3 fusion.14
  99.6 0.3 fusion.15
  100.0 0.3 fusion.17
  100.3 0.3 fusion.13
  100.7 0.3 fusion.18
  101.0 0.3 fusion.19
  101.4 0.3 fusion.20
  101.8 0.3 fusion.16
  102.1 2.0 fusion.10
  104.2 2.2 fusion.2
  106.4 1.0 fusion.101
  107.4 1.0 fusion.102
  108.3 0.4 fusion.46
  108.7 1.0 fusion.100
  109.7 11.7 %psum.21 = f32[1,512]{1,0:T(1,128)S(1)} all-reduce(f32[1,512]{1,0:T(1,128)S(1)} %bitcast.403), channel_id=1, replica_groups=mesh['dp'=32,'space'=4] {'space'}, use_global_device_ids=true, to_apply=%region_4.5 | all-reduce | flops 512 | bytes 4096 | tf_op jit(solution)/shard_map/psum | solution.py:87
  121.4 0.6 multiply_reduce_fusion
  123.4 63.9 %psum.22 = f32[]{:T(128)} all-reduce(f32[]{:T(128)} %sqrt.12), channel_id=1, replica_groups=mesh['dp'=32,'space'=4] {'dp'}, use_global_device_ids=true, to_apply=%region_6.7 | all-reduce | flops 1 | bytes 8 | tf_op jit(solution)/shard_map/psum | solution.py:89
  188.0 0.6 fusion.78
  188.6 1.8 fusion.80
  190.5 0.6 fusion.103
  191.1 7.3 %add_convert_fusion = (bf16[1,3,3,512,512]{4,3,2,1,0:T(8,128)(2,1)S(1)}, f32[512]{0:T(512)S(1)}) fusion(f32[1,3,3,512,512]{4,3,2,1,0:T(8,128)} %bitcast.338, f32[512]{0:T(512)S(1)} %fusion.94, f32[512]{0:T(512)S(1)} %bitcast.386, f32[512]{0:T(512)S(1)} %add_rsqrt_fusion, f32[512]{0:T(512)S(1)} %get-tuple-element.15, ...), kind=kLoop, calls=%fused_computation.22 | loop fusion | flops 40107520 | bytes 18884608 | tf_op jit(solution)/shard_map/jvp(vmap(jvp()))/convert_element_type | solution.py:36
  200.0 0.3 convolution_add_fusion.3
  200.4 0.3 convolution_add_fusion.2
  200.7 0.3 convolution_add_fusion.1
  201.0 0.3 fusion.35
  201.3 0.8 fusion.52
  202.1 0.3 fusion.21
  202.4 0.3 fusion.23
  202.8 0.3 fusion.24
  203.1 0.3 fusion.26
  203.5 0.3 fusion.22
  203.8 0.3 fusion.27
  204.2 0.3 fusion.28
  204.5 0.3 fusion.25
  204.9 0.3 fusion.29
  205.3 1.8 fusion.7
  207.4 7.7 %fusion.9 = bf16[3,3,512,512]{3,2,1,0:T(8,128)(2,1)} fusion(f32[3,3,32,16,512]{4,3,2,1,0:T(8,128)S(1)} %bitcast.340, f32[512,512]{1,0:T(8,128)S(1)} %multiply_add_fusion, f32[512]{0:T(512)S(1)} %fusion.94, f32[512]{0:T(512)S(1)} %bitcast.387, f32[512]{0:T(512)S(1)} %add_rsqrt_fusion, f32[512]{0:T(512)S(1)} %get-tuple-element.15, ...), kind=kLoop, calls=%fused_computation.18 | loop fusion | flops 68419584 | bytes 24649728 | tf_op jit(solution)/shard_map/convert_element_type | solution.py:109
  215.2 77.8 %reduce-scatter.2.cloned.1.call-done = bf16[3,3,16,512]{3,2,1,0:T(8,128)(2,1)} async-done(((bf16[3,3,512,512]{3,2,1,0:T(8,128)(2,1)}), bf16[3,3,16,512]{3,2,1,0:T(8,128)(2,1)}) %reduce-scatter.2.cloned.1.call-update) | async-done | bytes 147472 | tf_op jit(solution)/shard_map/reduce_scatter | solution.py:108
  293.0 43.3 %all-reduce.21.cloned.1.call-done = bf16[3,3,16,512]{3,2,1,0:T(8,128)(2,1)} async-done(((bf16[3,3,16,512]{3,2,1,0:T(8,128)(2,1)}), bf16[3,3,16,512]{3,2,1,0:T(8,128)(2,1)}) %all-reduce.21.cloned.1.call-update) | async-done | bytes 147472 | tf_op jit(solution)/shard_map/psum | solution.py:111
  336.2 1.7 convert_element_type.372
  (128 shorter events, 2.9 us)
Async XLA Ops:
  7.2 17.3 %copy-start = (f32[512,512]{1,0:T(8,128)S(1)}, f32[512,512]{1,0:T(8,128)}, u32[]{:S(2)}) copy-start(f32[512,512]{1,0:T(8,128)} %param.18) | copy-start | bytes 3145732
  10.9 7.8 %copy-start.16 = (bf16[1,2,128,512]{3,2,1,0:T(8,128)(2,1)S(1)}, bf16[1,2,128,512]{3,2,1,0:T(8,128)(2,1)}, u32[]{:S(2)}) copy-start(bf16[1,2,128,512]{3,2,1,0:T(8,128)(2,1)} %param.12) | copy-start | bytes 786436
  10.9 14.9 %copy-start.44 = (f32[512]{0:T(512)S(1)}, f32[512]{0:T(512)}, u32[]{:S(2)}) copy-start(f32[512]{0:T(512)} %param.19) | copy-start | bytes 6148
  10.9 14.9 %copy-start.42 = (f32[1,3,2,128]{3,2,1,0:T(2,128)S(1)}, f32[1,3,2,128]{3,2,1,0:T(2,128)}, u32[]{:S(2)}) copy-start(f32[1,3,2,128]{3,2,1,0:T(2,128)} %param.22) | copy-start | bytes 9220
  10.9 14.9 %copy-start.41 = (f32[512,3]{0,1:T(4,128)S(1)}, f32[512,3]{0,1:T(4,128)}, u32[]{:S(2)}) copy-start(f32[512,3]{0,1:T(4,128)} %param.20) | copy-start | bytes 18436
  10.9 16.0 %copy-start.17 = (f32[512,512]{1,0:T(8,128)S(1)}, f32[512,512]{1,0:T(8,128)}, u32[]{:S(2)}) copy-start(f32[512,512]{1,0:T(8,128)} %param.16) | copy-start | bytes 3145732
  10.9 17.4 %copy-start.45 = (f32[512]{0:T(512)S(1)}, f32[512]{0:T(512)}, u32[]{:S(2)}) copy-start(f32[512]{0:T(512)} %param.17) | copy-start | bytes 6148
  10.9 66.6 %all-to-all-start = ((bf16[32,3,3,16,512]{4,3,2,1,0:T(8,128)(2,1)}), bf16[32,3,3,16,512]{4,3,2,1,0:T(8,128)(2,1)}, u32[]{:S(2)}, u32[]{:S(2)}) async-start(bf16[32,3,3,16,512]{4,3,2,1,0:T(8,128)(2,1)} %stack.2), calls=%async_computation | async-start | bytes 9437184 | tf_op jit(solution)/shard_map/all_to_all | solution.py:70
  18.6 274.3 %reduce-scatter.2.cloned.1.call-start = ((), (), s32[]{:S(2)}) async-start(), calls=%async_computation.2 | async-start | bytes 4866048 | tf_op jit(solution)/shard_map/reduce_scatter | solution.py:108
  18.7 9.6 %collective-permute-start = (bf16[1,1,128,512]{3,2,1,0:T(8,128)(2,1)S(1)}, bf16[1,1,128,512]{3,2,1,0:T(8,128)(2,1)S(1)}, u32[]{:S(2)}, u32[]{:S(2)}) collective-permute-start(bf16[1,1,128,512]{3,2,1,0:T(8,128)(2,1)S(1)} %get-tuple-element.26), channel_id=1, source_target_pairs={{0,1},{1,2},{2,3},{4,5},{5,6},{6,7},{8,9},{9,10},{10,11},{12,13},{... | collective-permute-start | bytes 393224 | tf_op jit(solution)/shard_map/ppermute | solution.py:18
  22.5 7.4 %collective-permute-start.1 = (bf16[1,1,128,512]{3,2,1,0:T(8,128)(2,1)S(1)}, bf16[1,1,128,512]{3,2,1,0:T(8,128)(2,1)S(1)}, u32[]{:S(2)}, u32[]{:S(2)}) collective-permute-start(bf16[1,1,128,512]{3,2,1,0:T(8,128)(2,1)S(1)} %get-tuple-element.27), channel_id=1, source_target_pairs={{1,0},{2,1},{3,2},{5,4},{6,5},{7,6},{9,8},{10,9},{11,10},{13,12},{... | collective-permute-start | bytes 393224 | tf_op jit(solution)/shard_map/ppermute | solution.py:21
  31.9 63.7 %copy-start.22 = (bf16[1,2,128,512]{3,2,1,0:T(8,128)(2,1)}, bf16[1,2,128,512]{3,2,1,0:T(8,128)(2,1)S(1)}, u32[]{:S(2)}) copy-start(bf16[1,2,128,512]{3,2,1,0:T(8,128)(2,1)S(1)} %get-tuple-element.21) | copy-start | bytes 786436
  31.9 64.0 %copy-start.28 = (bf16[1,2,128,512]{3,2,1,0:T(8,128)(2,1)}, bf16[1,2,128,512]{3,2,1,0:T(8,128)(2,1)S(1)}, u32[]{:S(2)}) copy-start(bf16[1,2,128,512]{3,2,1,0:T(8,128)(2,1)S(1)} %get-tuple-element.20) | copy-start | bytes 786436
  31.9 64.9 %copy-start.19 = (bf16[1,2,128,512]{3,2,1,0:T(8,128)(2,1)}, bf16[1,2,128,512]{3,2,1,0:T(8,128)(2,1)S(1)}, u32[]{:S(2)}) copy-start(bf16[1,2,128,512]{3,2,1,0:T(8,128)(2,1)S(1)} %get-tuple-element.22) | copy-start | bytes 786436
  31.9 65.6 %copy-start.25 = (bf16[1,2,128,512]{3,2,1,0:T(8,128)(2,1)}, bf16[1,2,128,512]{3,2,1,0:T(8,128)(2,1)S(1)}, u32[]{:S(2)}) copy-start(bf16[1,2,128,512]{3,2,1,0:T(8,128)(2,1)S(1)} %get-tuple-element.18) | copy-start | bytes 786436
  93.9 10.2 %copy-start.1 = (f32[3,3,32,16,512]{4,3,2,1,0:T(8,128)}, f32[3,3,32,16,512]{4,3,2,1,0:T(8,128)S(1)}, u32[]{:S(2)}) copy-start(f32[3,3,32,16,512]{4,3,2,1,0:T(8,128)S(1)} %copy.23) | copy-start | bytes 28311556
  93.9 2.3 copy-start.31
  93.9 2.6 copy-start.33
  95.6 1.3 copy-start.43
  95.6 1.6 copy-start.35
  96.5 1.6 copy-start.37
  96.5 1.7 copy-start.39
  97.8 1.8 copy-start.29
  97.8 2.1 copy-start.26
  98.3 2.4 copy-start.23
  98.9 9.5 %copy-start.46 = (f32[256,512]{1,0:T(8,128)}, f32[256,512]{1,0:T(8,128)S(1)}, u32[]{:S(2)}) copy-start(f32[256,512]{1,0:T(8,128)S(1)} %get-tuple-element.29) | copy-start | bytes 1572868
  98.9 2.5 copy-start.20
  99.9 4.2 %copy-start.2 = (bf16[1,1,1,512,512]{4,3,2,1,0:T(8,128)(2,1)}, bf16[1,1,1,512,512]{4,3,2,1,0:T(8,128)(2,1)S(1)}, u32[]{:S(2)}) copy-start(bf16[1,1,1,512,512]{4,3,2,1,0:T(8,128)(2,1)S(1)} %fusion.15) | copy-start | bytes 1572868
  100.3 3.8 %copy-start.4 = (bf16[1,1,1,512,512]{4,3,2,1,0:T(8,128)(2,1)}, bf16[1,1,1,512,512]{4,3,2,1,0:T(8,128)(2,1)S(1)}, u32[]{:S(2)}) copy-start(bf16[1,1,1,512,512]{4,3,2,1,0:T(8,128)(2,1)S(1)} %fusion.17) | copy-start | bytes 1572868
  100.7 3.5 copy-start.6
  101.0 3.1 copy-start.8
  101.4 2.7 copy-start.10
  101.8 2.4 copy-start.12
  102.1 2.0 copy-start.14
  104.2 3.2 copy-start.18
  191.1 7.4 %copy-start.21 = (bf16[1,2,128,512]{3,2,1,0:T(8,128)(2,1)S(1)}, bf16[1,2,128,512]{3,2,1,0:T(8,128)(2,1)}, u32[]{:S(2)}) copy-start(bf16[1,2,128,512]{3,2,1,0:T(8,128)(2,1)} %copy-done.19) | copy-start | bytes 786436
  191.1 7.7 %copy-start.30 = (bf16[1,2,128,512]{3,2,1,0:T(8,128)(2,1)S(1)}, bf16[1,2,128,512]{3,2,1,0:T(8,128)(2,1)}, u32[]{:S(2)}) copy-start(bf16[1,2,128,512]{3,2,1,0:T(8,128)(2,1)} %copy-done.28) | copy-start | bytes 786436
  191.1 8.0 %copy-start.32 = (bf16[1,2,128,512]{3,2,1,0:T(8,128)(2,1)S(1)}, bf16[1,2,128,512]{3,2,1,0:T(8,128)(2,1)}, u32[]{:S(2)}) copy-start(bf16[1,2,128,512]{3,2,1,0:T(8,128)(2,1)} %get-tuple-element.19) | copy-start | bytes 786436
  191.1 8.3 %copy-start.34 = (bf16[1,2,128,512]{3,2,1,0:T(8,128)(2,1)S(1)}, bf16[1,2,128,512]{3,2,1,0:T(8,128)(2,1)}, u32[]{:S(2)}) copy-start(bf16[1,2,128,512]{3,2,1,0:T(8,128)(2,1)} %get-tuple-element.23) | copy-start | bytes 786436
  198.4 1.6 copy-start.36
  198.4 1.9 copy-start.24
  198.5 2.2 copy-start.27
  199.7 1.6 copy-start.38
  199.7 1.6 copy-start.40
  199.7 1.6 copy-start.47
  200.3 4.9 %slice-start = ((s8[9437184]{0:T(1024)(128)(4,1)}), s8[4194304]{0:T(1024)(128)(4,1)S(1)}, s32[]{:S(2)}) async-start(s8[9437184]{0:T(1024)(128)(4,1)} %bitcast.339), calls=%async_computation.4 | async-start | bytes 8388608
  201.3 3.9 %slice-start.1 = ((s8[9437184]{0:T(1024)(128)(4,1)}), s8[4194304]{0:T(1024)(128)(4,1)S(1)}, s32[]{:S(2)}) async-start(s8[9437184]{0:T(1024)(128)(4,1)} %bitcast.339), calls=%async_computation.5 | async-start | bytes 8388608
  202.4 2.8 slice-start.2
  205.3 2.1 copy-start.3
  205.3 2.1 copy-start.5
  205.3 2.1 copy-start.7
  205.3 2.1 copy-start.9
  205.3 2.1 copy-start.11
  205.3 2.1 copy-start.13
  205.3 2.1 copy-start.15
  215.1 121.1 %all-reduce.21.cloned.1.call-start = ((), (), s32[]{:S(2)}) async-start(), calls=%async_computation.3 | async-start | bytes 294912 | tf_op jit(solution)/shard_map/psum | solution.py:111
Sparse Core Ops, SparseCore 0:
  215.2 77.6 reduce-scatter.1
  295.4 40.8 all-reduce.20
